TPU v7x, 32 devices: a whole 2x2x4 slice. The times are simulated.
32 devices in a mesh: groups: 2 (over x), dp: 16 (over z, y, core).
Axes of the slice: x: 2, y: 2, z: 4, core: 2. Of those that a mesh axis runs over, the one named last changes fastest.
Arguments:
- tokens: bfloat16 [4096, 8192], P(('groups', 'dp')), parts along dimension 0, may hold values from -6 to 6
- output_gradient: bfloat16 [4096, 26624], P(('groups', 'dp')), parts along dimension 0, may hold values from -0.29882812 to 0.29882812
- adapter_down_factor: bfloat16 [16, 8192, 64], P('groups', 'dp'), parts along dimension 0, may hold values from -0.0625 to 0.0625
- adapter_up_factor: bfloat16 [16, 64, 26624], P('groups', None, 'dp'), parts along dimension 0, may hold values from -0.75 to 0.75
- job_row_counts: int32 [32, 8], P(('groups', 'dp')), parts along dimension 0, may hold values from 0 to 127, as said below
Outputs:
- grad_tokens: bfloat16 [4096, 8192], P(('groups', 'dp')), parts along dimension 0
- down_grad: float32 [16, 8192, 64], P('groups', 'dp'), parts along dimension 0
- up_grad: float32 [16, 64, 26624], P('groups', None, 'dp'), parts along dimension 0
There are 2 independent parts, one for each index of `groups`. A program takes and returns all parts, laid end to end along the dimension named above; each array names one. Nothing has to cross between parts.
Inputs may be any that keep to these rules, and one draw needn't show every extreme that they name: `job_row_counts`: every row has exactly two nonzero entries; their sum is at most 128 and equals 128 in at least one row.
All inputs are finite; a program needn't handle non-finite values.
Results may differ from a plain program's by a relative error of at most 0.008.
Values may be sent and summed in bfloat16 or wider, within the bound.
A program may use at most 128 MiB of HBM per device.

v0:
```python
import jax
import jax.numpy as jnp
from jax import lax
from jax.sharding import PartitionSpec as P

ADAPTER_SCALE = 2.0


def row_jobs(counts, row_count):
    ends = jnp.cumsum(counts, axis=1)
    starts = ends - counts
    position = jnp.arange(row_count, dtype=jnp.int32)[None, :, None]
    hot = (position >= starts[:, None, :]) & (position < ends[:, None, :])
    return hot.reshape(counts.shape[0] * row_count, counts.shape[1])


def local(tokens, output_gradient, down_factor, up_factor, counts):
    row_count = tokens.shape[0]
    n = lax.axis_size("dp")
    jobs, _, rank = down_factor.shape
    every_count = lax.all_gather(counts, "dp", axis=0, tiled=True)
    hot = row_jobs(every_count, row_count)
    grad_cols = lax.all_to_all(output_gradient, "dp", split_axis=1, concat_axis=0, tiled=True)
    token_cols = lax.all_to_all(tokens, "dp", split_axis=1, concat_axis=0, tiled=True)

    def select(terms):
        return jnp.sum(jnp.where(hot[:, :, None], terms, 0.0), axis=1)

    code_part = select(jnp.einsum("td,jdr->tjr", token_cols, down_factor, preferred_element_type=jnp.float32))
    grad_part = select(jnp.einsum("tc,jrc->tjr", grad_cols, up_factor, preferred_element_type=jnp.float32))
    parts = jnp.concatenate([code_part, grad_part], axis=1)
    parts = lax.all_to_all(parts, "dp", split_axis=0, concat_axis=0, tiled=True)
    own = jnp.sum(parts.reshape(n, row_count, 2 * rank), axis=0)
    own = jnp.concatenate([own[:, :rank], ADAPTER_SCALE * own[:, rank:]], axis=1).astype(jnp.bfloat16)
    whole = lax.all_gather(own, "dp", axis=0, tiled=True)

    def spread(rows):
        return jnp.where(hot[:, :, None], rows[:, None, :], jnp.bfloat16(0))

    codes, grads = spread(whole[:, :rank]), spread(whole[:, rank:])
    grad_token_cols = jnp.einsum("tjr,jdr->td", grads, down_factor, preferred_element_type=jnp.float32).astype(jnp.bfloat16)
    grad_tokens = lax.all_to_all(grad_token_cols, "dp", split_axis=0, concat_axis=1, tiled=True)
    down_grad = jnp.einsum("td,tjr->jdr", token_cols, grads, preferred_element_type=jnp.float32)
    up_grad = ADAPTER_SCALE * jnp.einsum("tjr,tc->jrc", codes, grad_cols, preferred_element_type=jnp.float32)
    return grad_tokens, down_grad, up_grad


def solution(mesh):
    return jax.shard_map(
        local,
        mesh=mesh,
        in_specs=(
            P(("groups", "dp"), None),
            P(("groups", "dp"), None),
            P("groups", "dp", None),
            P("groups", None, "dp"),
            P(("groups", "dp"), None),
        ),
        out_specs=(P(("groups", "dp"), None), P("groups", "dp", None), P("groups", None, "dp")),
        check_vma=False,
    )
```

profile of v0, /device:TPU:15, one launch (start us, length us, event | category | flops | bytes accessed | tf_op | source)
XLA Modules:
  0.0 341.6 jit_solution(9279513907533775807)
XLA Ops:
  0.6 0.0 copy-start
  0.6 3.3 copy.35
  3.9 6.6 %all-to-all-start = ((bf16[128,16,512]{2,0,1:T(8,128)(2,1)}), bf16[128,16,512]{2,0,1:T(8,128)(2,1)}, u32[]{:S(2)}, u32[]{:S(2)}) async-start(bf16[128,16,512]{2,0,1:T(8,128)(2,1)} %bitcast.57), calls=%async_computation | async-start | bytes 4194304 | tf_op jit(solution)/shard_map/all_to_all | solution.py:24
  10.5 6.6 %copy.34 = bf16[16,16,8,1664]{3,2,0,1:T(8,128)(2,1)} copy(bf16[16,16,8,1664]{3,2,1,0:T(8,128)(2,1)} %bitcast.58) | data formatting | bytes 13631488 | tf_op jit(solution)/shard_map/all_to_all | solution.py:23
  17.0 40.9 %all-to-all-done = bf16[128,16,512]{2,0,1:T(8,128)(2,1)} async-done(((bf16[128,16,512]{2,0,1:T(8,128)(2,1)}), bf16[128,16,512]{2,0,1:T(8,128)(2,1)}, u32[]{:S(2)}, u32[]{:S(2)}) %all-to-all-start) | async-done | bytes 2097184 | tf_op jit(solution)/shard_map/all_to_all | solution.py:24
  58.0 0.0 copy-start.2
  58.0 0.0 copy-start.1
  58.0 5.0 %all-to-all-start.1 = ((bf16[128,16,1664]{2,0,1:T(8,128)(2,1)}), bf16[128,16,1664]{2,0,1:T(8,128)(2,1)}, u32[]{:S(2)}, u32[]{:S(2)}) async-start(bf16[128,16,1664]{2,0,1:T(8,128)(2,1)} %bitcast.55), calls=%async_computation.1 | async-start | bytes 13631488 | tf_op jit(solution)/shard_map/all_to_all | solution.py:23
  63.0 0.0 copy-done.2
  63.0 157.9 %all-gather = s32[16,1,8]{2,1,0:T(1,128)S(1)} all-gather(s32[1,1,8]{2,1,0:T(1,128)S(1)} %bitcast.64), channel_id=1, replica_groups=mesh['groups'=2,'dp'=16] {'dp'}, dimensions={0}, use_global_device_ids=true | all-gather | bytes 544 | tf_op jit(solution)/shard_map/all_gather | solution.py:21
  220.9 0.1 copy.20
  221.0 0.1 copy.22
  221.1 0.1 copy.21
  221.2 0.1 fusion.16
  221.3 0.0 copy-done.1
  221.3 2.9 fusion.22
  224.2 0.5 select_reduce_fusion.1
  224.7 0.0 all-to-all-done.1
  224.7 0.0 copy-done
  224.7 7.2 %select_reduce_fusion = f32[2048,64]{0,1:T(8,128)S(1)} fusion(bf16[2048,1664,1]{1,0,2:T(8,128)(2,1)} %bitcast.12, bf16[8,64,1664]{2,1,0:T(8,128)(2,1)S(1)} %copy-done, pred[2048,8]{0,1:T(8,128)(4,1)S(1)} %fusion.16), kind=kOutput, calls=%fused_computation.2 | convolution fusion | flops 3491627008 | bytes 9060352 | tf_op jit(solution)/shard_map/tc,jrc->tjr/dot_general | solution.py:30
  231.9 0.1 copy_bitcast_fusion.2
  232.0 29.6 %all_to_all.66 = f32[16,128,128]{1,2,0:T(8,128)S(1)} all-to-all(f32[16,128,128]{1,2,0:T(8,128)S(1)} %copy_bitcast_fusion.2), channel_id=1, replica_groups=mesh['groups'=2,'dp'=16] {'dp'}, dimensions={0} | all-to-all | bytes 2097152 | tf_op jit(solution)/shard_map/all_to_all | solution.py:32
  261.6 0.1 reduce_sum.29
  261.7 16.5 %all_gather.7 = bf16[2048,128]{0,1:T(8,128)(2,1)S(1)} all-gather(bf16[128,128]{0,1:T(8,128)(2,1)S(1)} %pad_maximum_fusion), channel_id=1, replica_groups=mesh['groups'=2,'dp'=16] {'dp'}, dimensions={0}, use_global_device_ids=true | all-gather | bytes 557056 | tf_op jit(solution)/shard_map/all_gather | solution.py:35
  278.3 2.6 bitcast_convert_fusion
  280.9 10.0 %all-to-all-start.3 = ((bf16[16,128,512]{2,1,0:T(8,128)(2,1)}), bf16[16,128,512]{2,1,0:T(8,128)(2,1)}, u32[]{:S(2)}, u32[]{:S(2)}) async-start(bf16[16,128,512]{2,1,0:T(8,128)(2,1)} %bitcast.60), calls=%async_computation.3 | async-start | bytes 4194304 | tf_op jit(solution)/shard_map/all_to_all | solution.py:42
  290.9 3.8 %fusion.7 = f32[8,512,64]{1,2,0:T(8,128)} fusion(bf16[2048,512,1]{1,0,2:T(8,128)(2,1)} %bitcast.17, pred[2048,8]{0,1:T(8,128)(4,1)S(1)} %fusion.16, bf16[2048,64]{0,1:T(8,128)(2,1)S(1)} %get-tuple-element.4), kind=kOutput, calls=%fused_computation.13 | convolution fusion | flops 1074790400 | bytes 3424256 | tf_op jit(solution)/shard_map/td,tjr->jdr/dot_general | solution.py:43
  294.7 8.6 %convolution_multiply_fusion = f32[8,64,1664]{2,1,0:T(8,128)} fusion(bf16[2048,1664,1]{1,0,2:T(8,128)(2,1)} %bitcast.12, pred[2048,8]{0,1:T(8,128)(4,1)S(1)} %fusion.16, bf16[2048,64]{0,1:T(8,128)(2,1)S(1)} %get-tuple-element.3), kind=kOutput, calls=%fused_computation.4 | convolution fusion | flops 3491561472 | bytes 10502144 | tf_op jit(solution)/shard_map/tjr,tc->jrc/dot_general | solution.py:44
  303.4 35.1 %all-to-all-done.3 = bf16[16,128,512]{2,1,0:T(8,128)(2,1)} async-done(((bf16[16,128,512]{2,1,0:T(8,128)(2,1)}), bf16[16,128,512]{2,1,0:T(8,128)(2,1)}, u32[]{:S(2)}, u32[]{:S(2)}) %all-to-all-start.3) | async-done | bytes 2097184 | tf_op jit(solution)/shard_map/all_to_all | solution.py:42
  338.5 3.1 copy.30
  (7 shorter events, 0.1 us)
Async XLA Ops:
  0.6 224.1 %copy-start = (bf16[8,64,1664]{2,1,0:T(8,128)(2,1)S(1)}, bf16[8,64,1664]{2,1,0:T(8,128)(2,1)}, u32[]{:S(2)}) copy-start(bf16[8,64,1664]{2,1,0:T(8,128)(2,1)} %param.8) | copy-start | bytes 5111812
  3.9 54.1 %all-to-all-start = ((bf16[128,16,512]{2,0,1:T(8,128)(2,1)}), bf16[128,16,512]{2,0,1:T(8,128)(2,1)}, u32[]{:S(2)}, u32[]{:S(2)}) async-start(bf16[128,16,512]{2,0,1:T(8,128)(2,1)} %bitcast.57), calls=%async_computation | async-start | bytes 4194304 | tf_op jit(solution)/shard_map/all_to_all | solution.py:24
  58.0 5.0 %copy-start.2 = (s32[1,8]{1,0:T(1,128)S(1)}, s32[1,8]{1,0:T(1,128)}, u32[]{:S(2)}) copy-start(s32[1,8]{1,0:T(1,128)} %param.9) | copy-start | bytes 100
  58.0 163.3 %copy-start.1 = (bf16[8,512,64]{1,2,0:T(8,128)(2,1)S(1)}, bf16[8,512,64]{1,2,0:T(8,128)(2,1)}, u32[]{:S(2)}) copy-start(bf16[8,512,64]{1,2,0:T(8,128)(2,1)} %param.7) | copy-start | bytes 1572868
  58.0 166.7 %all-to-all-start.1 = ((bf16[128,16,1664]{2,0,1:T(8,128)(2,1)}), bf16[128,16,1664]{2,0,1:T(8,128)(2,1)}, u32[]{:S(2)}, u32[]{:S(2)}) async-start(bf16[128,16,1664]{2,0,1:T(8,128)(2,1)} %bitcast.55), calls=%async_computation.1 | async-start | bytes 13631488 | tf_op jit(solution)/shard_map/all_to_all | solution.py:23
  280.9 57.6 %all-to-all-start.3 = ((bf16[16,128,512]{2,1,0:T(8,128)(2,1)}), bf16[16,128,512]{2,1,0:T(8,128)(2,1)}, u32[]{:S(2)}, u32[]{:S(2)}) async-start(bf16[16,128,512]{2,1,0:T(8,128)(2,1)} %bitcast.60), calls=%async_computation.3 | async-start | bytes 4194304 | tf_op jit(solution)/shard_map/all_to_all | solution.py:42
where the time goes:
time: 342 us
  blocking collectives  204 us (60%)
  waiting for transfers between devices  76 us (22%)
  matrix products  25.1 us (7%)
  starting transfers between devices  21.6 us (6%)
  local copies, waits for them, and re-layouts  13.3 us (4%)
    all_gather x1, blocking collectives, local(): every_count = lax.all_gather(counts, 'dp', axis=0, tiled=True)  158 us
    all_to_all x1, waiting for transfers between devices, local(): lax.all_to_all(tokens, 'dp', split_axis=1, concat_axis=0, tiled=True)  40.9 us
    all_to_all x1, waiting for transfers between devices, local(): lax.all_to_all(grad_token_cols, 'dp', split_axis=0, concat_axis=1, tiled=...  35.1 us
    all_to_all x1, blocking collectives, local(): parts = lax.all_to_all(parts, 'dp', split_axis=0, concat_axis=0, tiled=True)  29.6 us
    all_gather x1, blocking collectives, local(): whole = lax.all_gather(own, 'dp', axis=0, tiled=True)  16.5 us
    all_to_all x1, starting transfers between devices, local(): lax.all_to_all(grad_token_cols, 'dp', split_axis=0, concat_axis=1, tiled=...  10 us
    dot_general x1, matrix products, local(): jnp.einsum('tjr,tc->jrc', codes, grad_cols, preferred_element_type=jnp.fl...  8.63 us
    dot_general x1, matrix products, local(): jnp.einsum('tc,jrc->tjr', grad_cols, up_factor, preferred_element_type=jn...  7.21 us
  transfers between devices with their start and end apart: 3, of which 2 were waited for; matrix products, arithmetic and copies ran while one was open for 7% of the time, Pallas kernels for 0%

commit v1 on v0

v1 whole, which is shorter than its diff:
```python
import functools

import jax
import jax.numpy as jnp
from jax import lax
from jax.experimental import pallas as pl
from jax.experimental.pallas import tpu as pltpu
from jax.sharding import PartitionSpec as P

ADAPTER_SCALE = 2.0
MESH = pl.DeviceIdType.MESH
F32 = jnp.float32
BF16 = jnp.bfloat16
NN = (((1,), (0,)), ((), ()))
NT = (((1,), (1,)), ((), ()))
TN = (((0,), (0,)), ((), ()))


def dot(a, b, dims):
    return lax.dot_general(a, b, dims, preferred_element_type=F32)


def kernel(
    n, split, tok, grad, down, up, spans, gt_out, dg_out, ug_out,
    g_cols, t_cols, a_all, s_all, code_all, rank_all, part_out, part_in, acc,
    own_sem, g_s, g_r, t_s, t_r, a_s, a_r, s_s, s_r, c_s, c_r, p_s, p_r, r_s, r_r,
):
    me = lax.axis_index("dp")
    rows = tok.shape[0]
    half = rows // 2
    d_cols = t_cols.shape[2]
    c_cols = g_cols.shape[2]
    pairs = s_all.shape[1] // 2

    def push(src, dst, send, recv, to):
        return pltpu.make_async_remote_copy(
            src_ref=src, dst_ref=dst, send_sem=send, recv_sem=recv,
            device_id={"dp": to}, device_id_type=MESH,
        )

    def others(body):
        def step(k, carry):
            body(k)
            return carry
        lax.fori_loop(1, n, step, 0)

    def ahead(k):
        return lax.rem(me + k, n)

    def behind(k):
        return lax.rem(me + n - k, n)

    def grad_slice(at):
        if split:
            return grad.at[at]
        return grad.at[:, pl.ds(pl.multiple_of(at * c_cols, 128), c_cols)]

    def tok_cols(at):
        return pl.ds(pl.multiple_of(at * d_cols, 128), d_cols)

    lane = lax.broadcasted_iota(jnp.int32, (half, 128), 1)
    place = lax.broadcasted_iota(jnp.int32, (rows, 128), 0)

    def mask(block, p):
        return (place >= s_all[block, p : p + 1, :]) & (place < s_all[block, pairs + p : pairs + p + 1, :])

    def fold(block, terms):
        total = jnp.zeros((rows, 128), F32)
        for p in range(pairs):
            total += jnp.where(mask(block, p), terms[:, 128 * p : 128 * (p + 1)], 0.0)
        twice = total + pltpu.roll(total, 64, 1)
        return jnp.where(lane < 64, twice[:half], twice[half:])

    def widen(block, packed):
        x = packed.astype(F32)
        y = pltpu.roll(x, 64, 1)
        both = jnp.concatenate([jnp.where(lane < 64, x, y), jnp.where(lane < 64, y, x)], axis=0)
        return jnp.concatenate([jnp.where(mask(block, p), both, 0.0) for p in range(pairs)], axis=1).astype(BF16)

    barrier = pltpu.get_barrier_semaphore()
    others(lambda k: pl.semaphore_signal(barrier, inc=1, device_id={"dp": ahead(k)}, device_id_type=MESH))
    s_all[me] = spans[...]
    a_all[me] = down[...]
    own = pltpu.make_async_copy(grad_slice(me), g_cols.at[me], own_sem)
    own.start()
    pl.semaphore_wait(barrier, n - 1)

    def span_copy(k):
        return push(s_all.at[me], s_all.at[me], s_s.at[k], s_r.at[me], ahead(k))

    def g_copy(k):
        return push(grad_slice(ahead(k)), g_cols.at[me], g_s.at[k], g_r.at[me], ahead(k))

    def t_copy(k):
        return push(tok.at[:, tok_cols(ahead(k))], t_cols.at[me], t_s.at[k], t_r.at[me], ahead(k))

    def code_copy(k):
        return push(code_all.at[me], code_all.at[me], c_s.at[k], c_r.at[me], ahead(k))

    def rank_copy(k):
        return push(rank_all.at[me], rank_all.at[me], r_s.at[k], r_r.at[me], ahead(k))

    def part_copy(k):
        return push(part_out.at[behind(k)], part_in.at[me], p_s.at[k], p_r.at[me], behind(k))

    def arrive(ref, recv, at):
        push(ref.at[at], ref.at[at], recv.at[at], recv.at[at], ahead(1)).wait_recv()

    others(lambda k: span_copy(k).start())
    bits = []
    m = n // 2
    while m:
        bits.append(m)
        m //= 2

    def a_copy(m, i):
        slot = lax.rem(me, 2 * m) + 2 * m * i
        at = n // (2 * m) - 1 + i
        mate = me + m - 2 * m * lax.rem(me // m, 2)
        return push(a_all.at[slot], a_all.at[slot], a_s.at[at], a_r.at[slot], mate)

    def each(lo, hi, body):
        def step(k, carry):
            body(k)
            return carry
        lax.fori_loop(lo, hi, step, 0)

    begun = 1
    for at, m in enumerate(bits):
        each(0, n // (2 * m), lambda i: a_copy(m, i).start())
        until = 1 + (n - 1) * (at + 1) // len(bits)
        each(begun, until, lambda k: g_copy(k).start())
        begun = until
        mate = me + m - 2 * m * lax.rem(me // m, 2)
        each(0, n // (2 * m), lambda i: arrive(a_all, a_r, lax.rem(mate, 2 * m) + 2 * m * i))

    t_cols[me] = tok[:, tok_cols(me)]

    acc[...] = jnp.zeros_like(acc)

    def code_step(s):
        acc[...] += dot(tok[:, tok_cols(s)], a_all[s], NN)
    each(0, n, code_step)
    code_all[me] = fold(me, acc[...]).astype(BF16)
    others(lambda k: code_copy(k).start())
    others(lambda k: arrive(s_all, s_r, behind(k)))

    def part_step(k):
        src = behind(k)
        arrive(g_cols, g_r, src)
        part_out[src] = fold(src, dot(g_cols[src], up[...], NT)).astype(BF16)
        part_copy(k).start()
        t_copy(k).start()
    others(part_step)
    own.wait()
    total0 = fold(me, dot(g_cols[me], up[...], NT))
    acc[:half, :128] = total0

    def sum_step(k):
        arrive(part_in, p_r, behind(k))
        acc[:half, :128] += part_in[behind(k)].astype(F32)
    others(sum_step)
    rank_all[me] = (ADAPTER_SCALE * acc[:half, :128]).astype(BF16)
    others(lambda k: rank_copy(k).start())

    wide = widen(me, rank_all[me])

    def gt_step(s):
        gt_out[:, tok_cols(s)] = dot(wide, a_all[s], NT).astype(BF16)
    each(0, n, gt_step)

    others(lambda k: arrive(code_all, c_r, behind(k)))
    ug_out[...] = jnp.zeros_like(ug_out)

    def ug_step(b):
        w = jnp.concatenate([widen(2 * b, code_all[2 * b]), widen(2 * b + 1, code_all[2 * b + 1])], axis=0)
        g = g_cols[pl.ds(2 * b, 2)].reshape(2 * rows, c_cols)
        ug_out[...] += dot(w, g, TN)
    each(0, n // 2, ug_step)

    others(lambda k: arrive(rank_all, r_r, behind(k)))
    others(lambda k: arrive(t_cols, t_r, behind(k)))
    dg_out[...] = jnp.zeros_like(dg_out)

    def dg_step(b):
        w = jnp.concatenate([widen(2 * b, rank_all[2 * b]), widen(2 * b + 1, rank_all[2 * b + 1])], axis=0)
        t = t_cols[pl.ds(2 * b, 2)].reshape(2 * rows, d_cols)
        dg_out[...] += dot(t, w, TN)
    each(0, n // 2, dg_step)

    for m in bits:
        each(0, n // (2 * m), lambda i: a_copy(m, i).wait_send())

    def drain(k):
        for make in (span_copy, g_copy, t_copy, code_copy, part_copy, rank_copy):
            make(k).wait_send()
    others(drain)


def local(tokens, output_gradient, down_factor, up_factor, counts):
    rows, features = tokens.shape
    hidden = output_gradient.shape[1]
    n = lax.axis_size("dp")
    jobs, d_cols, rank = down_factor.shape
    c_cols = up_factor.shape[2]
    wide = jobs * rank
    ends = jnp.cumsum(counts[0])
    starts = ends - counts[0]
    spans = jnp.repeat(jnp.concatenate([starts, ends]).astype(jnp.int32), rank).reshape(jobs, 2 * rank)
    down = down_factor.transpose(1, 0, 2).reshape(d_cols, wide)
    up = up_factor.reshape(wide, c_cols)
    split = c_cols % 128 != 0
    if split:
        output_gradient = output_gradient.reshape(rows, n, c_cols).transpose(1, 0, 2)
    vmem = pl.BlockSpec(memory_space=pltpu.VMEM)
    sems = pltpu.SemaphoreType.DMA((n,))
    packed = (n, rows // 2, 2 * rank)
    gt, dg, ug = pl.pallas_call(
        functools.partial(kernel, n, split),
        out_shape=(
            jax.ShapeDtypeStruct((rows, features), BF16),
            jax.ShapeDtypeStruct((d_cols, wide), F32),
            jax.ShapeDtypeStruct((wide, c_cols), F32),
        ),
        in_specs=[vmem, pl.BlockSpec(memory_space=pl.ANY), vmem, vmem, vmem],
        out_specs=(vmem, vmem, vmem),
        scratch_shapes=[
            pltpu.VMEM((n, rows, c_cols), BF16),
            pltpu.VMEM((n, rows, d_cols), BF16),
            pltpu.VMEM((n, d_cols, wide), BF16),
            pltpu.VMEM((n, jobs, 2 * rank), jnp.int32),
            pltpu.VMEM(packed, BF16),
            pltpu.VMEM(packed, BF16),
            pltpu.VMEM(packed, BF16),
            pltpu.VMEM(packed, BF16),
            pltpu.VMEM((rows, wide), F32),
            pltpu.SemaphoreType.DMA,
        ] + [sems] * 14,
        compiler_params=pltpu.CompilerParams(
            collective_id=0, has_side_effects=True, vmem_limit_bytes=56 * 1024 * 1024
        ),
    )(tokens, output_gradient, down, up, spans)
    down_grad = dg.reshape(d_cols, jobs, rank).transpose(1, 0, 2)
    up_grad = (ADAPTER_SCALE * ug).reshape(jobs, rank, c_cols)
    return gt, down_grad, up_grad


def solution(mesh):
    return jax.shard_map(
        local,
        mesh=mesh,
        in_specs=(
            P(("groups", "dp"), None),
            P(("groups", "dp"), None),
            P("groups", "dp", None),
            P("groups", None, "dp"),
            P(("groups", "dp"), None),
        ),
        out_specs=(P(("groups", "dp"), None), P("groups", "dp", None), P("groups", None, "dp")),
        check_vma=False,
    )
```

time: 342 us -> 291 us (0.85); the launches traced: 342 us -> 287 us
  Pallas kernels: 0 us -> 272 us
  blocking collectives: 204 us -> 0 us
  waiting for transfers between devices: 76 us -> 0 us
  matrix products: 25.1 us -> 0 us
  starting transfers between devices: 21.6 us -> 0 us
  other arithmetic: 0.82 us -> 6.91 us
  local copies, waits for them, and re-layouts: 13.3 us -> 7.33 us
    pallas_call x0 -> x1, Pallas kernels: none -> 272 us  [local(): pl.pallas_call(functools.partial(kernel, n, split), out_shape=(jax.ShapeD...]
    all_gather x2 -> x0, blocking collectives: 174 us -> none  [the longest x1 158 us: local(): every_count = lax.all_gather(counts, 'dp', axis=0, tiled=True)]
    all_to_all x3 -> x0, waiting for transfers between devices: 76 us -> none  [the longest x1 40.9 us: local(): lax.all_to_all(tokens, 'dp', split_axis=1, concat_axis=0, tiled=True)]
    all_to_all x1 -> x0, blocking collectives: 29.6 us -> none  [local(): parts = lax.all_to_all(parts, 'dp', split_axis=0, concat_axis=0, tiled=True)]
    dot_general x4 -> x0, matrix products: 22.3 us -> none  [the longest x1 8.63 us: local(): jnp.einsum('tjr,tc->jrc', codes, grad_cols, preferred_element_type=jnp.fl...]
    all_to_all x3 -> x0, starting transfers between devices: 21.6 us -> none  [the longest x1 10 us: local(): lax.all_to_all(grad_token_cols, 'dp', split_axis=0, concat_axis=1, tiled=...]
    all_to_all x3 -> x0, local copies, waits for them, and re-layouts: 13 us -> none  [the longest x1 6.58 us: local(): lax.all_to_all(output_gradient, 'dp', split_axis=1, concat_axis=0, tiled=...]
    mul x0 -> x1, other arithmetic: none -> 4.08 us  [local(): up_grad = (ADAPTER_SCALE * ug).reshape(jobs, rank, c_cols)]
  transfers between devices with their start and end apart: 3 -> 0, of which waited for: 2 -> 0; matrix products, arithmetic and copies ran while one was open for 7% -> 0% of each run, Pallas kernels for 0% -> 0%
where the time goes in v1:
time: 291 us; the launch traced here: 287 us
  Pallas kernels  272 us (93%)
  local copies, waits for them, and re-layouts  7.33 us (3%)
  other arithmetic  6.91 us (2%)
    pallas_call x1, Pallas kernels, local(): pl.pallas_call(functools.partial(kernel, n, split), out_shape=(jax.ShapeD...  272 us

profile of v1, /device:TPU:15, one launch (start us, length us, event | category | flops | bytes accessed | tf_op | source)
XLA Modules:
  0.0 287.1 jit_solution(12808236864492878884)
XLA Ops:
  0.6 0.8 reduce-window.6
  1.5 0.5 broadcast.7
  2.0 0.7 reduce.6
  2.6 1.3 reduce.7
  4.0 0.1 reshape.40
  4.0 0.1 squeeze.4
  4.1 0.1 broadcast_in_dim.5
  4.2 0.7 broadcast_in_dim.6.spans
  4.9 2.0 copy.17.down
  6.9 272.2 %shard_map.76 = (bf16[128,8192]{1,0:T(8,128)(2,1)}, f32[512,512]{1,0:T(8,128)}, f32[512,1664]{1,0:T(8,128)}) custom-call(bf16[128,8192]{1,0:T(8,128)(2,1)} %tok.1, bf16[128,26624]{1,0:T(8,128)(2,1)} %grad.1, bf16[512,512]{1,0:T(8,128)(2,1)} %copy.17.down, bf16[512,1664]{1,0:T(8,128)(2,1)} %bitcast.11, s32[8,128]{1,0:T(8,128)} %broadcast_in_dim.6.spans), custom_call_target="tpu_custom_call" | custom-call | tf_op jit(solution)/shard_map/pallas_call | solution.py:218
  279.1 2.5 copy.18
  281.7 0.0 copy-start
  281.7 4.1 %broadcast_multiply_fusion = f32[512,1664]{1,0:T(8,128)} fusion(f32[512,1664]{1,0:T(8,128)} %get-tuple-element.8), kind=kLoop, calls=%fused_computation | loop fusion | flops 851968 | bytes 6815744 | tf_op jit(solution)/shard_map/mul | solution.py:244
  285.8 0.0 copy-done
  285.8 1.3 copy.20
  (2 shorter events, 0.0 us)
Async XLA Ops:
  281.7 4.1 %copy-start = (bf16[128,8192]{1,0:T(8,128)(2,1)S(1)}, bf16[128,8192]{1,0:T(8,128)(2,1)}, u32[]{:S(2)}) copy-start(bf16[128,8192]{1,0:T(8,128)(2,1)} %get-tuple-element.12) | copy-start | bytes 6291460

commit v2 on v1

--- a/solution.py
+++ b/solution.py
@@ -21,7 +21,7 @@
 
 
 def kernel(
-    n, split, tok, grad, down, up, spans, gt_out, dg_out, ug_out,
+    n, split, tok, grad, down, up, counts, gt_out, dg_out, ug_out,
     g_cols, t_cols, a_all, s_all, code_all, rank_all, part_out, part_in, acc,
     own_sem, g_s, g_r, t_s, t_r, a_s, a_r, s_s, s_r, c_s, c_r, p_s, p_r, r_s, r_r,
 ):
@@ -44,11 +44,21 @@
             return carry
         lax.fori_loop(1, n, step, 0)
 
+    def flip(a, b):
+        total, bit = 0, 1
+        while bit < n:
+            total += lax.rem(a // bit + b // bit, 2) * bit
+            bit *= 2
+        return total
+
     def ahead(k):
-        return lax.rem(me + k, n)
-
-    def behind(k):
-        return lax.rem(me + n - k, n)
+        i = k - 1
+        odd = lax.rem(i, 2)
+        side = lax.rem(me, 2)
+        far = lax.rem(odd + side + 1, 2)
+        return flip(me, far * (n // 2) + (i + odd) // 2 + side * (1 - odd))
+
+    behind = ahead
 
     def grad_slice(at):
         if split:
@@ -77,9 +87,18 @@
         both = jnp.concatenate([jnp.where(lane < 64, x, y), jnp.where(lane < 64, y, x)], axis=0)
         return jnp.concatenate([jnp.where(mask(block, p), both, 0.0) for p in range(pairs)], axis=1).astype(BF16)
 
+    other = lax.rem(me + 1, n)
     barrier = pltpu.get_barrier_semaphore()
     others(lambda k: pl.semaphore_signal(barrier, inc=1, device_id={"dp": ahead(k)}, device_id_type=MESH))
-    s_all[me] = spans[...]
+    row = lax.broadcasted_iota(jnp.int32, (2 * pairs, 128), 0)
+    side = lax.broadcasted_iota(jnp.int32, (2 * pairs, 128), 1) // 64
+    spans = jnp.zeros((2 * pairs, 128), jnp.int32)
+    at = jnp.int32(0)
+    for j in range(2 * pairs):
+        spans = jnp.where((row == j // 2) & (side == j % 2), at, spans)
+        at = at + counts[0, j]
+        spans = jnp.where((row == pairs + j // 2) & (side == j % 2), at, spans)
+    s_all[me] = spans
     a_all[me] = down[...]
     own = pltpu.make_async_copy(grad_slice(me), g_cols.at[me], own_sem)
     own.start()
@@ -104,7 +123,7 @@
         return push(part_out.at[behind(k)], part_in.at[me], p_s.at[k], p_r.at[me], behind(k))
 
     def arrive(ref, recv, at):
-        push(ref.at[at], ref.at[at], recv.at[at], recv.at[at], ahead(1)).wait_recv()
+        push(ref.at[at], ref.at[at], recv.at[at], recv.at[at], other).wait_recv()
 
     others(lambda k: span_copy(k).start())
     bits = []
@@ -128,7 +147,7 @@
     begun = 1
     for at, m in enumerate(bits):
         each(0, n // (2 * m), lambda i: a_copy(m, i).start())
-        until = 1 + (n - 1) * (at + 1) // len(bits)
+        until = 1 + min(n - 1, (n - 1) * (at + 1) // max(1, len(bits) - 1))
         each(begun, until, lambda k: g_copy(k).start())
         begun = until
         mate = me + m - 2 * m * lax.rem(me // m, 2)
@@ -139,7 +158,7 @@
     acc[...] = jnp.zeros_like(acc)
 
     def code_step(s):
-        acc[...] += dot(tok[:, tok_cols(s)], a_all[s], NN)
+        acc[...] += dot(tok[:, tok_cols(s)], a_all[s], NT)
     each(0, n, code_step)
     code_all[me] = fold(me, acc[...]).astype(BF16)
     others(lambda k: code_copy(k).start())
@@ -166,7 +185,7 @@
     wide = widen(me, rank_all[me])
 
     def gt_step(s):
-        gt_out[:, tok_cols(s)] = dot(wide, a_all[s], NT).astype(BF16)
+        gt_out[:, tok_cols(s)] = dot(wide, a_all[s], NN).astype(BF16)
     each(0, n, gt_step)
 
     others(lambda k: arrive(code_all, c_r, behind(k)))
@@ -185,7 +204,7 @@
     def dg_step(b):
         w = jnp.concatenate([widen(2 * b, rank_all[2 * b]), widen(2 * b + 1, rank_all[2 * b + 1])], axis=0)
         t = t_cols[pl.ds(2 * b, 2)].reshape(2 * rows, d_cols)
-        dg_out[...] += dot(t, w, TN)
+        dg_out[...] += dot(w, t, TN)
     each(0, n // 2, dg_step)
 
     for m in bits:
@@ -204,10 +223,7 @@
     jobs, d_cols, rank = down_factor.shape
     c_cols = up_factor.shape[2]
     wide = jobs * rank
-    ends = jnp.cumsum(counts[0])
-    starts = ends - counts[0]
-    spans = jnp.repeat(jnp.concatenate([starts, ends]).astype(jnp.int32), rank).reshape(jobs, 2 * rank)
-    down = down_factor.transpose(1, 0, 2).reshape(d_cols, wide)
+    down = down_factor.transpose(0, 2, 1).reshape(wide, d_cols)
     up = up_factor.reshape(wide, c_cols)
     split = c_cols % 128 != 0
     if split:
@@ -219,15 +235,15 @@
         functools.partial(kernel, n, split),
         out_shape=(
             jax.ShapeDtypeStruct((rows, features), BF16),
-            jax.ShapeDtypeStruct((d_cols, wide), F32),
+            jax.ShapeDtypeStruct((wide, d_cols), F32),
             jax.ShapeDtypeStruct((wide, c_cols), F32),
         ),
-        in_specs=[vmem, pl.BlockSpec(memory_space=pl.ANY), vmem, vmem, vmem],
+        in_specs=[vmem, pl.BlockSpec(memory_space=pl.ANY), vmem, vmem, pl.BlockSpec(memory_space=pltpu.SMEM)],
         out_specs=(vmem, vmem, vmem),
         scratch_shapes=[
             pltpu.VMEM((n, rows, c_cols), BF16),
             pltpu.VMEM((n, rows, d_cols), BF16),
-            pltpu.VMEM((n, d_cols, wide), BF16),
+            pltpu.VMEM((n, wide, d_cols), BF16),
             pltpu.VMEM((n, jobs, 2 * rank), jnp.int32),
             pltpu.VMEM(packed, BF16),
             pltpu.VMEM(packed, BF16),
@@ -239,8 +255,8 @@
         compiler_params=pltpu.CompilerParams(
             collective_id=0, has_side_effects=True, vmem_limit_bytes=56 * 1024 * 1024
         ),
-    )(tokens, output_gradient, down, up, spans)
-    down_grad = dg.reshape(d_cols, jobs, rank).transpose(1, 0, 2)
+    )(tokens, output_gradient, down, up, counts)
+    down_grad = dg.reshape(jobs, rank, d_cols).transpose(0, 2, 1)
     up_grad = (ADAPTER_SCALE * ug).reshape(jobs, rank, c_cols)
     return gt, down_grad, up_grad
 

time: 291 us -> 270 us (0.928)
  Pallas kernels: 272 us -> 261 us
  local copies, waits for them, and re-layouts: 7.33 us -> 2.93 us
    pallas_call x1, Pallas kernels: 272 us -> 261 us  [local(): pl.pallas_call(functools.partial(kernel, n, split), out_shape=(jax.ShapeD...]
where the time goes in v2:
time: 270 us; the launch traced here: 268 us
  Pallas kernels  261 us (97%)
  other arithmetic  4.08 us (2%)
  local copies, waits for them, and re-layouts  2.93 us (1%)
    pallas_call x1, Pallas kernels, local(): pl.pallas_call(functools.partial(kernel, n, split), out_shape=(jax.ShapeD...  261 us

profile of v2, /device:TPU:15, one launch (start us, length us, event | category | flops | bytes accessed | tf_op | source)
XLA Modules:
  0.0 268.3 jit_solution(4807162227413054499)
XLA Ops:
  0.6 260.7 %shard_map.76 = (bf16[128,8192]{1,0:T(8,128)(2,1)}, f32[512,512]{1,0:T(8,128)}, f32[512,1664]{1,0:T(8,128)}) custom-call(bf16[128,8192]{1,0:T(8,128)(2,1)} %tok.1, bf16[128,26624]{1,0:T(8,128)(2,1)} %grad.1, bf16[512,512]{1,0:T(8,128)(2,1)} %bitcast.11, bf16[512,1664]{1,0:T(8,128)(2,1)} %bitcast.9, s32[1,8]{1,0:T(1,128)} %counts.1), custom_call_target="tpu_custom_call" | custom-call | tf_op jit(solution)/shard_map/pallas_call | solution.py:234
  261.3 0.0 copy-start
  261.3 4.1 %broadcast_multiply_fusion = f32[512,1664]{1,0:T(8,128)} fusion(f32[512,1664]{1,0:T(8,128)} %get-tuple-element.8), kind=kLoop, calls=%fused_computation | loop fusion | flops 851968 | bytes 6815744 | tf_op jit(solution)/shard_map/mul | solution.py:260
  265.4 0.0 copy-start.1
  265.4 0.0 copy-done
  265.4 1.3 copy.10
  266.7 0.6 copy-done.1
  267.4 1.0 copy.11
Async XLA Ops:
  261.3 4.1 %copy-start = (bf16[128,8192]{1,0:T(8,128)(2,1)S(1)}, bf16[128,8192]{1,0:T(8,128)(2,1)}, u32[]{:S(2)}) copy-start(bf16[128,8192]{1,0:T(8,128)(2,1)} %get-tuple-element.12) | copy-start | bytes 6291460
  265.4 2.0 copy-start.1

commit v3 on v2

--- a/solution.py
+++ b/solution.py
@@ -169,8 +169,14 @@
         arrive(g_cols, g_r, src)
         part_out[src] = fold(src, dot(g_cols[src], up[...], NT)).astype(BF16)
         part_copy(k).start()
+
+    def both_step(k):
+        part_step(k)
         t_copy(k).start()
-    others(part_step)
+    soon, later = n * 8 // 16, n * 12 // 16
+    each(1, soon, both_step)
+    each(soon, n, part_step)
+    each(soon, later, lambda k: t_copy(k).start())
     own.wait()
     total0 = fold(me, dot(g_cols[me], up[...], NT))
     acc[:half, :128] = total0
@@ -181,6 +187,7 @@
     others(sum_step)
     rank_all[me] = (ADAPTER_SCALE * acc[:half, :128]).astype(BF16)
     others(lambda k: rank_copy(k).start())
+    each(later, n, lambda k: t_copy(k).start())
 
     wide = widen(me, rank_all[me])
 

time: 270 us -> 264 us (0.978)
  Pallas kernels: 261 us -> 254 us
    pallas_call x1, Pallas kernels: 261 us -> 254 us  [local(): pl.pallas_call(functools.partial(kernel, n, split), out_shape=(jax.ShapeD...]
where the time goes in v3:
time: 264 us; the launch traced here: 262 us
  Pallas kernels  254 us (96%)
  other arithmetic  4.08 us (2%)
  local copies, waits for them, and re-layouts  2.93 us (1%)
    pallas_call x1, Pallas kernels, local(): pl.pallas_call(functools.partial(kernel, n, split), out_shape=(jax.ShapeD...  254 us

profile of v3, /device:TPU:15, one launch (start us, length us, event | category | flops | bytes accessed | tf_op | source)
XLA Modules:
  0.0 261.8 jit_solution(2584154655760537388)
XLA Ops:
  0.6 254.1 %shard_map.76 = (bf16[128,8192]{1,0:T(8,128)(2,1)}, f32[512,512]{1,0:T(8,128)}, f32[512,1664]{1,0:T(8,128)}) custom-call(bf16[128,8192]{1,0:T(8,128)(2,1)} %tok.1, bf16[128,26624]{1,0:T(8,128)(2,1)} %grad.1, bf16[512,512]{1,0:T(8,128)(2,1)} %bitcast.11, bf16[512,1664]{1,0:T(8,128)(2,1)} %bitcast.9, s32[1,8]{1,0:T(1,128)} %counts.1), custom_call_target="tpu_custom_call" | custom-call | tf_op jit(solution)/shard_map/pallas_call | solution.py:241
  254.7 0.0 copy-start
  254.8 4.1 %broadcast_multiply_fusion = f32[512,1664]{1,0:T(8,128)} fusion(f32[512,1664]{1,0:T(8,128)} %get-tuple-element.8), kind=kLoop, calls=%fused_computation | loop fusion | flops 851968 | bytes 6815744 | tf_op jit(solution)/shard_map/mul | solution.py:267
  258.8 0.0 copy-start.1
  258.8 0.0 copy-done
  258.8 1.3 copy.10
  260.2 0.6 copy-done.1
  260.8 1.0 copy.11
Async XLA Ops:
  254.7 4.1 %copy-start = (bf16[128,8192]{1,0:T(8,128)(2,1)S(1)}, bf16[128,8192]{1,0:T(8,128)(2,1)}, u32[]{:S(2)}) copy-start(bf16[128,8192]{1,0:T(8,128)(2,1)} %get-tuple-element.12) | copy-start | bytes 6291460
  258.8 2.0 copy-start.1
